TPU v7x, 32 devices: a whole 2x2x4 slice. The times are simulated.
32 devices in a mesh: dp: 8 (over z, y), tensor: 4 (over x, core).
Axes of the slice: x: 2, y: 2, z: 4, core: 2. Of those that a mesh axis runs over, the one named last changes fastest.
Arguments:
- cotangent: bfloat16 [2048, 4096], P('dp'), may hold values from -0.375 to 0.375
- activations: bfloat16 [2048, 4096], P('dp', 'tensor'), may hold values from -6 to 6
- error_buf: bfloat16 [8, 4096, 4096], P('dp', None, 'tensor'), may hold values from -6 to 6
- q_start: float32 [32, 4096], P(None, 'tensor'), may hold values from -6 to 6
Outputs:
- basis: float32 [32, 4096], replicated
- q_factor: float32 [32, 4096], P(None, 'tensor')
All inputs are finite; a program needn't handle non-finite values.
Results may differ from a plain program's by a relative error of at most 0.0003.
Values sent between devices are 32-bit elements; how exact they have to be, the bound alone decides.
A program may use at most 128 MiB of HBM per device.

v0:
```python
import jax
import jax.numpy as jnp
from jax import lax
from jax.sharding import PartitionSpec as P

POWER = 2


def lower_inverse(gram):
    lower = jnp.linalg.cholesky(gram)
    return jax.scipy.linalg.solve_triangular(
        lower, jnp.eye(gram.shape[0], dtype=jnp.float32), lower=True
    )


def on_device(cotangent, activations, error_buf, q_start):
    high = lax.Precision.HIGHEST
    carried = error_buf[0]
    gradient = lax.dot_general(
        cotangent, activations, (((0,), (0,)), ((), ())), preferred_element_type=jnp.float32
    )
    fed = gradient + carried.astype(jnp.float32)
    q_now = q_start
    p_hat = None
    for number in range(POWER):
        p_sum = lax.psum(
            lax.dot_general(q_now, fed, (((1,), (1,)), ((), ())), precision=high), ("dp", "tensor")
        )
        gram = jnp.dot(p_sum, p_sum.T, precision=high)
        p_hat = jnp.dot(lower_inverse(gram), p_sum, precision=high)
        q_now = lax.psum(jnp.dot(p_hat, fed, precision=high), "dp")
    basis = jnp.sqrt(jnp.float32(p_hat.shape[1])) * p_hat
    return (basis, q_now / lax.axis_size("dp"))


def solution(mesh):
    return jax.shard_map(
        on_device,
        mesh=mesh,
        in_specs=(P("dp", None), P("dp", "tensor"), P("dp", None, "tensor"), P(None, "tensor")),
        out_specs=(P(), P(None, "tensor")),
        check_vma=False,
    )
```

profile of v0, /device:TPU:0, one launch (start us, length us, event | category | flops | bytes accessed | tf_op | source)
XLA Modules:
  0.0 508.8 jit_solution(18087185005112340681)
XLA Ops:
  7.2 0.0 copy-start
  7.2 0.0 copy-start.2
  7.2 0.0 all-reduce.5.cloned.1.call-start
  7.2 1.5 copy-done
  8.8 6.0 %convert_add_fusion = f32[4096,1024]{1,0:T(8,128)S(1)} fusion(bf16[256,4096]{1,0:T(8,128)(2,1)S(1)} %copy-done, bf16[256,1024]{1,0:T(8,128)(2,1)} %param.8, bf16[1,4096,1024]{2,1,0:T(8,128)(2,1)} %param.9), kind=kOutput, calls=%fused_computation | convolution fusion | flops 2155872256 | bytes 27787264 | tf_op jit(solution)/shard_map/dot_general | solution.py:19
  14.7 0.0 copy-start.1
  14.7 5.7 %copy-done.1 = f32[4096,1024]{1,0:T(8,128)} copy-done((f32[4096,1024]{1,0:T(8,128)}, f32[4096,1024]{1,0:T(8,128)S(1)}, u32[]{:S(2)}) %copy-start.1) | copy-done | bytes 16777240
  20.4 0.0 copy-done.2
  20.4 16.3 %convolution_bitcast_fusion = f32[32,4096]{1,0:T(8,128)} fusion(f32[4096,1024]{1,0:T(8,128)S(1)} %convert_add_fusion, f32[32,1024]{1,0:T(8,128)S(1)} %copy-done.2), kind=kOutput, calls=%fused_computation.1 | convolution fusion | flops 1610612736 | bytes 17432576 | tf_op jit(solution)/shard_map/dot_general | solution.py:27
  36.8 0.0 all-reduce.5.cloned.1.call-update
  36.8 0.0 all-reduce.7.cloned.1.call-start
  36.8 130.7 %all-reduce.5.cloned.1.call-done = f32[32,4096]{1,0:T(8,128)} async-done(((f32[32,4096]{1,0:T(8,128)}), f32[32,4096]{1,0:T(8,128)}) %all-reduce.5.cloned.1.call-update) | async-done | bytes 524304 | tf_op jit(solution)/shard_map/psum | solution.py:26
  167.5 1.8 fusion.12
  169.2 0.1 copy.6
  169.3 2.9 cholesky.44
  172.3 0.6 compare_reduce_fusion.1
  172.9 0.7 fusion.4
  173.6 2.4 custom-call.6
  176.0 0.2 fusion.2
  176.3 1.6 fusion.13
  177.9 13.8 %fusion.14 = f32[32,1024]{1,0:T(8,128)} fusion(f32[32,4096]{1,0:T(8,128)S(1)} %fusion.13, f32[4096,1024]{1,0:T(8,128)} %copy-done.1), kind=kOutput, calls=%fused_computation.27 | convolution fusion | flops 1610612736 | bytes 17432576 | tf_op jit(solution)/shard_map/dot_general | solution.py:31
  191.6 0.0 all-reduce.7.cloned.1.call-update
  191.7 0.3 all-reduce.9.cloned.1.call-start
  191.9 68.5 %all-reduce.7.cloned.1.call-done = f32[32,1024]{1,0:T(8,128)} async-done(((f32[32,1024]{1,0:T(8,128)}), f32[32,1024]{1,0:T(8,128)}) %all-reduce.7.cloned.1.call-update) | async-done | bytes 131088 | tf_op jit(solution)/shard_map/psum | solution.py:31
  260.5 19.2 %fusion.15 = f32[32,4096]{1,0:T(8,128)} fusion(f32[32,1024]{1,0:T(8,128)} %all-reduce.7.cloned.1.call-done, f32[4096,1024]{1,0:T(8,128)} %copy-done.1), kind=kOutput, calls=%fused_computation.28 | convolution fusion | flops 1610612736 | bytes 17432576 | tf_op jit(solution)/shard_map/dot_general | solution.py:27
  279.6 0.0 all-reduce.9.cloned.1.call-update
  279.7 0.0 all-reduce.11.cloned.1.call-start
  279.7 127.2 %all-reduce.9.cloned.1.call-done = f32[32,4096]{1,0:T(8,128)} async-done(((f32[32,4096]{1,0:T(8,128)}), f32[32,4096]{1,0:T(8,128)}) %all-reduce.9.cloned.1.call-update) | async-done | bytes 524304 | tf_op jit(solution)/shard_map/psum | solution.py:26
  406.9 1.8 fusion.16
  408.7 0.1 copy.7
  408.8 2.9 cholesky.55
  411.7 0.6 compare_reduce_fusion
  412.4 0.7 fusion.5
  413.0 2.4 custom-call.7
  415.5 0.2 fusion
  415.7 2.4 broadcast_multiply_fusion
  418.1 13.8 %fusion.17 = f32[32,1024]{1,0:T(8,128)} fusion(f32[32,4096]{1,0:T(8,128)S(1)} %get-tuple-element.5, f32[4096,1024]{1,0:T(8,128)} %copy-done.1), kind=kOutput, calls=%fused_computation.30 | convolution fusion | flops 1610612736 | bytes 17432576 | tf_op jit(solution)/shard_map/dot_general | solution.py:31
  431.9 0.0 all-reduce.11.cloned.1.call-update
  431.9 68.8 %all-reduce.11.cloned.1.call-done = f32[32,1024]{1,0:T(8,128)} async-done(((f32[32,1024]{1,0:T(8,128)}), f32[32,1024]{1,0:T(8,128)}) %all-reduce.11.cloned.1.call-update) | async-done | bytes 131088 | tf_op jit(solution)/shard_map/psum | solution.py:31
  500.7 1.6 broadcast_multiply_fusion.1
  (4 shorter events, 0.1 us)
Async XLA Ops:
  7.2 1.6 copy-start
  7.2 13.3 %copy-start.2 = (f32[32,1024]{1,0:T(8,128)S(1)}, f32[32,1024]{1,0:T(8,128)}, u32[]{:S(2)}) copy-start(f32[32,1024]{1,0:T(8,128)} %param.10) | copy-start | bytes 393220
  7.2 160.3 %all-reduce.5.cloned.1.call-start = ((), (), s32[]{:S(2)}) async-start(), calls=%async_computation | async-start | bytes 1048576 | tf_op jit(solution)/shard_map/psum | solution.py:26
  14.7 5.7 %copy-start.1 = (f32[4096,1024]{1,0:T(8,128)}, f32[4096,1024]{1,0:T(8,128)S(1)}, u32[]{:S(2)}) copy-start(f32[4096,1024]{1,0:T(8,128)S(1)} %convert_add_fusion) | copy-start | bytes 50331652
  36.8 223.7 %all-reduce.7.cloned.1.call-start = ((), (), s32[]{:S(2)}) async-start(), calls=%async_computation.1 | async-start | bytes 262144 | tf_op jit(solution)/shard_map/psum | solution.py:31
  191.7 215.3 %all-reduce.9.cloned.1.call-start = ((), (), s32[]{:S(2)}) async-start(), calls=%async_computation.2 | async-start | bytes 1048576 | tf_op jit(solution)/shard_map/psum | solution.py:26
  279.7 221.0 %all-reduce.11.cloned.1.call-start = ((), (), s32[]{:S(2)}) async-start(), calls=%async_computation.3 | async-start | bytes 262144 | tf_op jit(solution)/shard_map/psum | solution.py:31
Sparse Core Ops, SparseCore 0:
  36.9 130.5 all-reduce.4
  191.8 68.6 all-reduce.6
  279.8 127.1 all-reduce.8
  432.0 68.6 all-reduce.10
where the time goes:
time: 509 us
  waiting for transfers between devices  395 us (78%)
  matrix products  77 us (15%)
  other arithmetic  14.9 us (3%)
  between operations  13.9 us (3%)
  local copies, waits for them, and re-layouts  7.39 us (1%)
    psum x2, waiting for transfers between devices, on_device(): lax.psum(lax.dot_general(q_now, fed, (((1,), (1,)), ((), ())), precision=...  258 us
    psum x2, waiting for transfers between devices, on_device(): q_now = lax.psum(jnp.dot(p_hat, fed, precision=high), 'dp')  137 us
    dot_general x2, matrix products, on_device(): lax.dot_general(q_now, fed, (((1,), (1,)), ((), ())), precision=high)  35.5 us
    dot_general x2, matrix products, on_device(): q_now = lax.psum(jnp.dot(p_hat, fed, precision=high), 'dp')  27.5 us
  transfers between devices with their start and end apart: 4, of which 4 were waited for; matrix products, arithmetic and copies ran while one was open for 0% of the time, Pallas kernels for 0%

commit v1 on v0

v1 whole, which is shorter than its diff:
```python
import functools

import jax
import jax.numpy as jnp
from jax import lax
from jax.experimental import pallas as pl
from jax.experimental.pallas import tpu as pltpu
from jax.sharding import PartitionSpec as P

POWER = 2
LANES = 128
NT = (((1,), (1,)), ((), ()))
NN = (((1,), (0,)), ((), ()))
HIGH = lax.Precision.HIGHEST


def lower_inverse(gram):
    lower = jnp.linalg.cholesky(gram)
    return jax.scipy.linalg.solve_triangular(
        lower, jnp.eye(gram.shape[0], dtype=jnp.float32), lower=True
    )


def plain(cotangent, activations, error_buf, q_start):
    carried = error_buf[0]
    gradient = lax.dot_general(
        cotangent, activations, (((0,), (0,)), ((), ())), preferred_element_type=jnp.float32
    )
    fed = gradient + carried.astype(jnp.float32)
    q_now = q_start
    p_hat = None
    for number in range(POWER):
        p_sum = lax.psum(lax.dot_general(q_now, fed, NT, precision=HIGH), ("dp", "tensor"))
        gram = jnp.dot(p_sum, p_sum.T, precision=HIGH)
        p_hat = jnp.dot(lower_inverse(gram), p_sum, precision=HIGH)
        q_now = lax.psum(jnp.dot(p_hat, fed, precision=HIGH), "dp")
    basis = jnp.sqrt(jnp.float32(p_hat.shape[1])) * p_hat
    return (basis, q_now / lax.axis_size("dp"))


def pieces3(x):
    first = x.astype(jnp.bfloat16)
    rest = x - first.astype(jnp.float32)
    second = rest.astype(jnp.bfloat16)
    third = (rest - second.astype(jnp.float32)).astype(jnp.bfloat16)
    return jnp.concatenate([first, second, third], axis=0)


def folded(x):
    n = x.shape[0] // 3
    return (x[2 * n :] + x[n : 2 * n]) + x[:n]


def dot(a, b, dims):
    return lax.dot_general(a, b, dims, preferred_element_type=jnp.float32)


def inverse_factor(gram):
    n = gram.shape[0]
    row = lax.broadcasted_iota(jnp.int32, (n, n), 0)
    column = lax.broadcasted_iota(jnp.int32, (n, n), 1)
    inverse = jnp.where(row == column, 1.0, 0.0).astype(jnp.float32)
    for j in range(n - 1):
        lead = gram[j : j + 1, :]
        ratio = gram[:, j : j + 1] / gram[j : j + 1, j : j + 1]
        factor = jnp.where(row > j, jnp.broadcast_to(ratio, (n, n)), 0.0)
        gram = gram - factor * lead
        inverse = inverse - factor * inverse[j : j + 1, :]
    pivot = jnp.sum(jnp.where(row == column, gram, 0.0), axis=1, keepdims=True)
    root = lax.rsqrt(pivot)
    root = root * (1.5 - 0.5 * ((pivot * root) * root))
    return inverse * root


def kernel(
    replicas, scale,
    cot_hbm, act_hbm, err_hbm, q_hbm, p_out, q_out,
    cot, act, err, q_first, q3,
    send_a, take_a, send_b, take_b, send_c, take_c, full,
    acc, acc_u, acc_g, q_part, q_take, q_full,
    load_sem, a_s, a_r, b_s, b_r, c_s, c_r, d_s, d_r, e_s, e_r, f_s, f_r, g_s, g_r, h_s, h_r,
):
    dp, tensor = lax.axis_index("dp"), lax.axis_index("tensor")
    z, y = dp // 2, dp % 2
    x, core = tensor // 2, tensor % 2
    other = 1 - core
    width = err.shape[2]
    blocks = width // LANES

    def plane(j):
        return (x + j // 2) % 2, (y + j % 2) % 2

    def plane_at(j):
        px, py = plane(j)
        return px * 2 + py

    def plane_device(j):
        px, py = plane(j)
        return (z * 2 + py, px * 2 + core)

    def column_device(k):
        return (((z + k) % 4) * 2 + y, tensor)

    core_device = (dp, x * 2 + other)

    def replica_device(k):
        return ((dp + k) % replicas, tensor)

    order = (1, 2, 3, 0)

    loads = [
        pltpu.make_async_copy(q_hbm, q_first, load_sem.at[0]),
        pltpu.make_async_copy(act_hbm, act, load_sem.at[1]),
        pltpu.make_async_copy(cot_hbm, cot, load_sem.at[2]),
    ]
    err_loads = {}
    for h, half in enumerate((other, core)):
        for n, j in enumerate(order):
            err_loads[h, j] = pltpu.make_async_copy(
                err_hbm.at[half, plane_at(j)], err.at[half, plane_at(j)], load_sem.at[3 + h * 4 + n]
            )
    for copy in loads:
        copy.start()
    for copy in err_loads.values():
        copy.start()

    barrier = pltpu.get_barrier_semaphore()
    partners = [core_device]
    partners += [plane_device(j) for j in (1, 2, 3)]
    partners += [column_device(k) for k in (1, 2, 3)]
    partners += [(((z + k) % 4) * 2 + (1 - y), tensor) for k in (1, 2, 3)]
    for device in partners:
        pl.semaphore_signal(barrier, inc=1, device_id=device, device_id_type=pl.DeviceIdType.MESH)

    def remote(src, dst, send, take, device):
        copy = pltpu.make_async_remote_copy(
            src_ref=src, dst_ref=dst, send_sem=send, recv_sem=take,
            device_id=device, device_id_type=pl.DeviceIdType.MESH,
        )
        copy.start()
        return copy

    for number in range(POWER):
        last = number == POWER - 1
        if number == 0:
            loads[0].wait()
            q_now = q_first[...]
        else:
            q_now = jnp.concatenate([q_full[i] for i in range(replicas)], axis=1)
        q3[...] = pieces3(q_now)
        if number == 0:
            loads[1].wait()
        through3 = pieces3(folded(dot(q3[...], act[...], NT)))
        if number == 0:
            loads[2].wait()

        def row_term(h, half, j):
            at = plane_at(j)
            if number == 0:
                err_loads[h, j].wait()
            columns = pl.ds(pl.multiple_of((half * 4 + at) * width, width), width)
            return folded(
                dot(q3[...], err[half, at], NT) + dot(through3, cot[:, columns], NN)
            )

        sends = []
        core_sums = {}
        for j in order:
            term = row_term(0, other, j)
            for b in range(blocks):
                send_a[j, b] = term[:, b * LANES : (b + 1) * LANES]
            if number == 0 and j == order[0]:
                pl.semaphore_wait(barrier, len(partners))
            core_sums[j] = remote(send_a.at[j], take_a.at[j], a_s.at[j], a_r.at[j], core_device)
        sends += list(core_sums.values())
        plane_sums = {}
        for j in order:
            term = row_term(1, core, j)
            core_sums[j].wait_recv()
            for b in range(blocks):
                send_b[j, b] = term[:, b * LANES : (b + 1) * LANES] + take_a[j, b]
            if j:
                plane_sums[j] = remote(send_b.at[j], take_b.at[j], b_s.at[j], b_r.at[j], plane_device(j))
        sends += list(plane_sums.values())
        for j in (1, 2, 3):
            plane_sums[j].wait_recv()
        for b in range(blocks):
            send_c[b] = (send_b[0, b] + take_b[1, b]) + (take_b[2, b] + take_b[3, b])
        column_sums = [
            remote(send_c.at[(z + k) % 4], take_c.at[k], c_s.at[k], c_r.at[k], column_device(k))
            for k in (1, 2, 3)
        ]
        sends += column_sums
        for copy in column_sums:
            copy.wait_recv()
        mine = plane_at(0)
        full[core, mine, z] = (send_c[z] + take_c[1]) + (take_c[2] + take_c[3])

        block = full.at[core, mine, z]
        column_full = [
            remote(block, block, d_s.at[k], d_r.at[k], column_device(k)) for k in (1, 2, 3)
        ]
        sends += column_full
        for copy in column_full:
            copy.wait_recv()
        piece = full.at[core, mine]
        plane_full = {
            j: remote(piece, piece, e_s.at[j], e_r.at[j], plane_device(j)) for j in (1, 2, 3)
        }
        sends += list(plane_full.values())
        core_full = {0: remote(piece, piece, f_s.at[0], f_r.at[0], core_device)}

        def column_term(half, j, first):
            at = plane_at(j)
            p3 = pieces3(jnp.concatenate([full[half, at, b] for b in range(blocks)], axis=1))
            columns = pl.ds(pl.multiple_of((half * 4 + at) * width, width), width)
            by_err = dot(p3, err[half, at], NN)
            by_cot = dot(p3, cot[:, columns], NT)
            by_self = dot(p3, p3, NT)
            if first:
                acc[...] = by_err
                acc_u[...] = by_cot
                acc_g[...] = by_self
            else:
                acc[...] += by_err
                acc_u[...] += by_cot
                acc_g[...] += by_self

        column_term(core, 0, True)
        for j in (1, 2, 3):
            plane_full[j].wait_recv()
            got = full.at[core, plane_at(j)]
            core_full[j] = remote(got, got, f_s.at[j], f_r.at[j], core_device)
            column_term(core, j, False)
        for j in range(4):
            core_full[j].wait_recv()
            column_term(other, j, False)
        sends += list(core_full.values())

        q_sum = folded(acc[...]) + folded(dot(pieces3(folded(acc_u[...])), act[...], NN))
        for i in range(replicas):
            q_part[i] = q_sum[:, i * LANES : (i + 1) * LANES]
        q_sums = [
            remote(q_part.at[(dp + k) % replicas], q_take.at[k], g_s.at[k], g_r.at[k], replica_device(k))
            for k in range(1, replicas)
        ]
        sends += q_sums
        rank = q_sum.shape[0]
        g_rows = folded(acc_g[...])
        gram = (g_rows[:, 2 * rank :] + g_rows[:, rank : 2 * rank]) + g_rows[:, :rank]
        inverse = inverse_factor(gram)
        total = q_part[dp]
        for k, copy in enumerate(q_sums):
            copy.wait_recv()
            total = total + q_take[k + 1]
        q_own = jnp.dot(inverse, total, precision=HIGH, preferred_element_type=jnp.float32)
        if last:
            q_own = q_own / replicas
        q_full[dp] = q_own
        q_back = [
            remote(q_full.at[dp], q_full.at[dp], h_s.at[k], h_r.at[k], replica_device(k))
            for k in range(1, replicas)
        ]
        sends += q_back
        if last:
            for half in range(2):
                for at in range(4):
                    p_sum = jnp.concatenate([full[half, at, b] for b in range(blocks)], axis=1)
                    p_hat = jnp.dot(inverse, p_sum, precision=HIGH, preferred_element_type=jnp.float32)
                    start = (half * 4 + at) * width
                    p_out[:, start : start + width] = p_hat * scale
        for copy in q_back:
            copy.wait_recv()
        if last:
            for i in range(replicas):
                q_out[:, i * LANES : (i + 1) * LANES] = q_full[i]
        for copy in sends:
            copy.wait_send()


def fits(replicas, shards, tokens, rows, columns, rank):
    return replicas == 8 and shards == 4 and rows == 32 * LANES and columns == replicas * LANES and rank % 16 == 0


def solution(mesh):
    replicas, shards = mesh.shape["dp"], mesh.shape["tensor"]

    def on_device(cotangent, activations, error_buf, q_start):
        tokens, rows = cotangent.shape
        rank, columns = q_start.shape
        if not fits(replicas, shards, tokens, rows, columns, rank):
            return plain(cotangent, activations, error_buf, q_start)
        width = rows // 8
        blocks = width // LANES
        f32 = jnp.float32
        dma = pltpu.SemaphoreType.DMA
        any_space = pl.BlockSpec(memory_space=pl.ANY)
        vmem = pl.BlockSpec(memory_space=pltpu.VMEM)
        sems = [dma((11,))]
        for count in (4, 4, 4, 4, 4, 4, replicas, replicas):
            sems += [dma((count,)), dma((count,))]
        return pl.pallas_call(
            functools.partial(kernel, replicas, float(rows) ** 0.5),
            out_shape=(
                jax.ShapeDtypeStruct((rank, rows), f32),
                jax.ShapeDtypeStruct((rank, columns), f32),
            ),
            in_specs=[any_space] * 4,
            out_specs=(vmem, vmem),
            scratch_shapes=[
                pltpu.VMEM((tokens, rows), jnp.bfloat16),
                pltpu.VMEM((tokens, columns), jnp.bfloat16),
                pltpu.VMEM((2, 4, width, columns), jnp.bfloat16),
                pltpu.VMEM((rank, columns), f32),
                pltpu.VMEM((3 * rank, columns), jnp.bfloat16),
                pltpu.VMEM((4, blocks, rank, LANES), f32),
                pltpu.VMEM((4, blocks, rank, LANES), f32),
                pltpu.VMEM((4, blocks, rank, LANES), f32),
                pltpu.VMEM((4, blocks, rank, LANES), f32),
                pltpu.VMEM((blocks, rank, LANES), f32),
                pltpu.VMEM((4, rank, LANES), f32),
                pltpu.VMEM((2, 4, blocks, rank, LANES), f32),
                pltpu.VMEM((3 * rank, columns), f32),
                pltpu.VMEM((3 * rank, tokens), f32),
                pltpu.VMEM((3 * rank, 3 * rank), f32),
                pltpu.VMEM((replicas, rank, LANES), f32),
                pltpu.VMEM((replicas, rank, LANES), f32),
                pltpu.VMEM((replicas, rank, LANES), f32),
            ]
            + sems,
            compiler_params=pltpu.CompilerParams(
                collective_id=0, has_side_effects=True, vmem_limit_bytes=48 * 1024 * 1024
            ),
        )(cotangent, activations, error_buf.reshape(2, 4, width, columns), q_start)

    return jax.shard_map(
        on_device,
        mesh=mesh,
        in_specs=(P("dp", None), P("dp", "tensor"), P("dp", None, "tensor"), P(None, "tensor")),
        out_specs=(P(), P(None, "tensor")),
        check_vma=False,
    )
```

time: 509 us -> 79.7 us (0.16)
  waiting for transfers between devices: 395 us -> 0 us
  matrix products: 77 us -> 0 us
  Pallas kernels: 0 us -> 73.8 us
  other arithmetic: 14.9 us -> 0 us
  between operations: 13.9 us -> 0.65 us
    psum x4 -> x0, waiting for transfers between devices: 395 us -> none  [the longest x2 258 us: on_device(): lax.psum(lax.dot_general(q_now, fed, (((1,), (1,)), ((), ())), precision=...]
    dot_general x9 -> x0, matrix products: 76.5 us -> none  [the longest x2 35.5 us: on_device(): lax.dot_general(q_now, fed, (((1,), (1,)), ((), ())), precision=high)]
    pallas_call x0 -> x1, Pallas kernels: none -> 73.8 us  [on_device(): pl.pallas_call(functools.partial(kernel, replicas, float(rows) ** 0.5), o...]
    another operation x10 -> x0, other arithmetic: 13.4 us -> none  [the longest x6 7.19 us: lower_inverse(): lower = jnp.linalg.cholesky(gram)]
  transfers between devices with their start and end apart: 4 -> 0, of which waited for: 4 -> 0; matrix products, arithmetic and copies ran while one was open for 0% -> 0% of each run, Pallas kernels for 0% -> 0%
where the time goes in v1:
time: 79.7 us; the launch traced here: 79.5 us
  Pallas kernels  73.8 us (93%)
  local copies, waits for them, and re-layouts  4.98 us (6%)
    pallas_call x1, Pallas kernels, on_device(): pl.pallas_call(functools.partial(kernel, replicas, float(rows) ** 0.5), o...  73.8 us
    unnamed x8, local copies, waits for them, and re-layouts  4.98 us

profile of v1, /device:TPU:0, one launch (start us, length us, event | category | flops | bytes accessed | tf_op | source)
XLA Modules:
  0.0 79.5 jit_solution(13574645764823134384)
XLA Ops:
  0.6 0.0 copy-start
  0.6 1.6 %copy-done = bf16[256,4096]{1,0:T(8,128)(2,1)S(1)} copy-done((bf16[256,4096]{1,0:T(8,128)(2,1)S(1)}, bf16[256,4096]{1,0:T(8,128)(2,1)}, u32[]{:S(2)}) %copy-start) | copy-done | bytes 2097176
  2.2 0.0 copy-start.1
  2.2 1.0 %copy-done.1 = bf16[256,1024]{1,0:T(8,128)(2,1)S(1)} copy-done((bf16[256,1024]{1,0:T(8,128)(2,1)S(1)}, bf16[256,1024]{1,0:T(8,128)(2,1)}, u32[]{:S(2)}) %copy-start.1) | copy-done | bytes 524312
  3.3 0.0 copy-start.2
  3.3 0.9 %copy-done.2 = f32[32,1024]{1,0:T(8,128)S(1)} copy-done((f32[32,1024]{1,0:T(8,128)S(1)}, f32[32,1024]{1,0:T(8,128)}, u32[]{:S(2)}) %copy-start.2) | copy-done | bytes 131096
  4.2 73.8 %shard_map.59 = (f32[32,4096]{1,0:T(8,128)S(1)}, f32[32,1024]{1,0:T(8,128)S(1)}) custom-call(bf16[256,4096]{1,0:T(8,128)(2,1)S(1)} %copy-done, bf16[256,1024]{1,0:T(8,128)(2,1)S(1)} %copy-done.1, bf16[2,4,512,1024]{3,2,1,0:T(8,128)(2,1)} %bitcast.1, f32[32,1024]{1,0:T(8,128)S(1)} %copy-done.2), custom_call_target="tpu_custom_call" | custom-call | tf_op jit(solution)/shard_map/pallas_call | solution.py:302
  78.0 0.8 %copy.8 = f32[32,4096]{1,0:T(8,128)} copy(f32[32,4096]{1,0:T(8,128)S(1)} %get-tuple-element.4) | data formatting | bytes 1048576
  78.8 0.7 copy.9
Async XLA Ops:
  0.6 1.6 %copy-start = (bf16[256,4096]{1,0:T(8,128)(2,1)S(1)}, bf16[256,4096]{1,0:T(8,128)(2,1)}, u32[]{:S(2)}) copy-start(bf16[256,4096]{1,0:T(8,128)(2,1)} %cot_hbm.1) | copy-start | bytes 6291460
  2.2 1.0 %copy-start.1 = (bf16[256,1024]{1,0:T(8,128)(2,1)S(1)}, bf16[256,1024]{1,0:T(8,128)(2,1)}, u32[]{:S(2)}) copy-start(bf16[256,1024]{1,0:T(8,128)(2,1)} %act_hbm.1) | copy-start | bytes 1572868
  3.3 0.9 %copy-start.2 = (f32[32,1024]{1,0:T(8,128)S(1)}, f32[32,1024]{1,0:T(8,128)}, u32[]{:S(2)}) copy-start(f32[32,1024]{1,0:T(8,128)} %q_hbm.1) | copy-start | bytes 393220

commit v2 on v1

--- a/solution.py
+++ b/solution.py
@@ -76,9 +76,9 @@
     replicas, scale,
     cot_hbm, act_hbm, err_hbm, q_hbm, p_out, q_out,
     cot, act, err, q_first, q3,
-    send_a, take_a, send_b, take_b, send_c, take_c, full,
+    send_a, take_a, send_b, take_b, full,
     acc, acc_u, acc_g, q_part, q_take, q_full,
-    load_sem, a_s, a_r, b_s, b_r, c_s, c_r, d_s, d_r, e_s, e_r, f_s, f_r, g_s, g_r, h_s, h_r,
+    load_sem, a_s, a_r, b_s, b_r, c_s, c_r, f_s, f_r, g_s, g_r, h_s, h_r,
 ):
     dp, tensor = lax.axis_index("dp"), lax.axis_index("tensor")
     z, y = dp // 2, dp % 2
@@ -94,12 +94,9 @@
         px, py = plane(j)
         return px * 2 + py
 
-    def plane_device(j):
+    def chip_device(j, k):
         px, py = plane(j)
-        return (z * 2 + py, px * 2 + core)
-
-    def column_device(k):
-        return (((z + k) % 4) * 2 + y, tensor)
+        return (((z + k) % 4) * 2 + py, px * 2 + core)
 
     core_device = (dp, x * 2 + other)
 
@@ -107,6 +104,7 @@
         return ((dp + k) % replicas, tensor)
 
     order = (1, 2, 3, 0)
+    far = (2, 1, 3, 0)
 
     loads = [
         pltpu.make_async_copy(q_hbm, q_first, load_sem.at[0]),
@@ -126,9 +124,7 @@
 
     barrier = pltpu.get_barrier_semaphore()
     partners = [core_device]
-    partners += [plane_device(j) for j in (1, 2, 3)]
-    partners += [column_device(k) for k in (1, 2, 3)]
-    partners += [(((z + k) % 4) * 2 + (1 - y), tensor) for k in (1, 2, 3)]
+    partners += [chip_device(j, k) for j in range(4) for k in range(4) if j or k]
     for device in partners:
         pl.semaphore_signal(barrier, inc=1, device_id=device, device_id_type=pl.DeviceIdType.MESH)
 
@@ -173,42 +169,36 @@
                 pl.semaphore_wait(barrier, len(partners))
             core_sums[j] = remote(send_a.at[j], take_a.at[j], a_s.at[j], a_r.at[j], core_device)
         sends += list(core_sums.values())
-        plane_sums = {}
+        chip_sums = []
         for j in order:
             term = row_term(1, core, j)
             core_sums[j].wait_recv()
             for b in range(blocks):
                 send_b[j, b] = term[:, b * LANES : (b + 1) * LANES] + take_a[j, b]
-            if j:
-                plane_sums[j] = remote(send_b.at[j], take_b.at[j], b_s.at[j], b_r.at[j], plane_device(j))
-        sends += list(plane_sums.values())
-        for j in (1, 2, 3):
-            plane_sums[j].wait_recv()
-        for b in range(blocks):
-            send_c[b] = (send_b[0, b] + take_b[1, b]) + (take_b[2, b] + take_b[3, b])
-        column_sums = [
-            remote(send_c.at[(z + k) % 4], take_c.at[k], c_s.at[k], c_r.at[k], column_device(k))
-            for k in (1, 2, 3)
-        ]
-        sends += column_sums
-        for copy in column_sums:
+            for k in far:
+                if j or k:
+                    n = j * 4 + k
+                    chip_sums.append(
+                        remote(send_b.at[j, (z + k) % 4], take_b.at[n], b_s.at[n], b_r.at[n], chip_device(j, k))
+                    )
+        sends += chip_sums
+        mine = plane_at(0)
+        total = send_b[0, z]
+        for copy in chip_sums:
             copy.wait_recv()
-        mine = plane_at(0)
-        full[core, mine, z] = (send_c[z] + take_c[1]) + (take_c[2] + take_c[3])
+        for n in range(1, 16):
+            total = total + take_b[n]
+        full[core, mine, z] = total
 
         block = full.at[core, mine, z]
-        column_full = [
-            remote(block, block, d_s.at[k], d_r.at[k], column_device(k)) for k in (1, 2, 3)
-        ]
-        sends += column_full
-        for copy in column_full:
-            copy.wait_recv()
-        piece = full.at[core, mine]
-        plane_full = {
-            j: remote(piece, piece, e_s.at[j], e_r.at[j], plane_device(j)) for j in (1, 2, 3)
-        }
-        sends += list(plane_full.values())
-        core_full = {0: remote(piece, piece, f_s.at[0], f_r.at[0], core_device)}
+        chip_full = {}
+        for j in (0, 1, 2, 3):
+            for k in far:
+                if j or k:
+                    n = j * 4 + k
+                    chip_full[j, k] = remote(block, block, c_s.at[n], c_r.at[n], chip_device(j, k))
+        sends += list(chip_full.values())
+        core_full = {}
 
         def column_term(half, j, first):
             at = plane_at(j)
@@ -226,12 +216,13 @@
                 acc_u[...] += by_cot
                 acc_g[...] += by_self
 
-        column_term(core, 0, True)
-        for j in (1, 2, 3):
-            plane_full[j].wait_recv()
+        for j in range(4):
+            for k in far:
+                if j or k:
+                    chip_full[j, k].wait_recv()
             got = full.at[core, plane_at(j)]
             core_full[j] = remote(got, got, f_s.at[j], f_r.at[j], core_device)
-            column_term(core, j, False)
+            column_term(core, j, j == 0)
         for j in range(4):
             core_full[j].wait_recv()
             column_term(other, j, False)
@@ -297,7 +288,7 @@
         any_space = pl.BlockSpec(memory_space=pl.ANY)
         vmem = pl.BlockSpec(memory_space=pltpu.VMEM)
         sems = [dma((11,))]
-        for count in (4, 4, 4, 4, 4, 4, replicas, replicas):
+        for count in (4, 16, 16, 4, replicas, replicas):
             sems += [dma((count,)), dma((count,))]
         return pl.pallas_call(
             functools.partial(kernel, replicas, float(rows) ** 0.5),
@@ -316,9 +307,7 @@
                 pltpu.VMEM((4, blocks, rank, LANES), f32),
                 pltpu.VMEM((4, blocks, rank, LANES), f32),
                 pltpu.VMEM((4, blocks, rank, LANES), f32),
-                pltpu.VMEM((4, blocks, rank, LANES), f32),
-                pltpu.VMEM((blocks, rank, LANES), f32),
-                pltpu.VMEM((4, rank, LANES), f32),
+                pltpu.VMEM((16, rank, LANES), f32),
                 pltpu.VMEM((2, 4, blocks, rank, LANES), f32),
                 pltpu.VMEM((3 * rank, columns), f32),
                 pltpu.VMEM((3 * rank, tokens), f32),
@@ -329,7 +318,7 @@
             ]
             + sems,
             compiler_params=pltpu.CompilerParams(
-                collective_id=0, has_side_effects=True, vmem_limit_bytes=48 * 1024 * 1024
+                collective_id=0, has_side_effects=True, vmem_limit_bytes=60 * 1024 * 1024
             ),
         )(cotangent, activations, error_buf.reshape(2, 4, width, columns), q_start)
 

time: 79.7 us -> 72.2 us (0.906)
  Pallas kernels: 73.8 us -> 68 us
  local copies, waits for them, and re-layouts: 4.98 us -> 3.44 us
    pallas_call x1, Pallas kernels: 73.8 us -> 68 us  [on_device(): pl.pallas_call(functools.partial(kernel, replicas, float(rows) ** 0.5), o...]
    unnamed x8 -> x2, local copies, waits for them, and re-layouts: 4.98 us -> 3.44 us
where the time goes in v2:
time: 72.2 us; the launch traced here: 72.1 us
  Pallas kernels  68 us (94%)
  local copies, waits for them, and re-layouts  3.44 us (5%)
    pallas_call x1, Pallas kernels, on_device(): pl.pallas_call(functools.partial(kernel, replicas, float(rows) ** 0.5), o...  68 us
    unnamed x2, local copies, waits for them, and re-layouts  3.44 us

profile of v2, /device:TPU:0, one launch (start us, length us, event | category | flops | bytes accessed | tf_op | source)
XLA Modules:
  0.0 72.1 jit_solution(9977763610377723391)
XLA Ops:
  0.6 68.0 %shard_map.59 = (f32[32,4096]{1,0:T(8,128)}, f32[32,1024]{1,0:T(8,128)}) custom-call(bf16[256,4096]{1,0:T(8,128)(2,1)} %cot_hbm.1, bf16[256,1024]{1,0:T(8,128)(2,1)} %act_hbm.1, bf16[2,4,512,1024]{3,2,1,0:T(8,128)(2,1)} %bitcast.1, f32[32,1024]{1,0:T(8,128)} %q_hbm.1), custom_call_target="tpu_custom_call" | custom-call | tf_op jit(solution)/shard_map/pallas_call | solution.py:293
  68.6 1.9 %copy.8 = f32[32,4096]{1,0:T(8,128)} copy(f32[32,4096]{1,0:T(8,128)} %get-tuple-element.4) | data formatting | bytes 1048576
  70.5 1.6 %copy.9 = f32[32,1024]{1,0:T(8,128)} copy(f32[32,1024]{1,0:T(8,128)} %get-tuple-element.5) | data formatting | bytes 262144

commit v3 on v2

--- a/solution.py
+++ b/solution.py
@@ -269,6 +269,11 @@
             copy.wait_send()
 
 
+def hand_out(p_in, q_in, p_out, q_out):
+    p_out[...] = p_in[...]
+    q_out[...] = q_in[...]
+
+
 def fits(replicas, shards, tokens, rows, columns, rank):
     return replicas == 8 and shards == 4 and rows == 32 * LANES and columns == replicas * LANES and rank % 16 == 0
 
@@ -290,12 +295,13 @@
         sems = [dma((11,))]
         for count in (4, 16, 16, 4, replicas, replicas):
             sems += [dma((count,)), dma((count,))]
-        return pl.pallas_call(
+        shapes = (
+            jax.ShapeDtypeStruct((rank, rows), f32),
+            jax.ShapeDtypeStruct((rank, columns), f32),
+        )
+        found = pl.pallas_call(
             functools.partial(kernel, replicas, float(rows) ** 0.5),
-            out_shape=(
-                jax.ShapeDtypeStruct((rank, rows), f32),
-                jax.ShapeDtypeStruct((rank, columns), f32),
-            ),
+            out_shape=shapes,
             in_specs=[any_space] * 4,
             out_specs=(vmem, vmem),
             scratch_shapes=[
@@ -321,6 +327,12 @@
                 collective_id=0, has_side_effects=True, vmem_limit_bytes=60 * 1024 * 1024
             ),
         )(cotangent, activations, error_buf.reshape(2, 4, width, columns), q_start)
+        return pl.pallas_call(
+            hand_out,
+            out_shape=shapes,
+            in_specs=[vmem] * 2,
+            out_specs=(vmem, vmem),
+        )(*found)
 
     return jax.shard_map(
         on_device,

time: 72.2 us -> 70.7 us (0.979)
  local copies, waits for them, and re-layouts: 3.44 us -> 0 us
  Pallas kernels: 68 us -> 69.9 us
    unnamed x2 -> x0, local copies, waits for them, and re-layouts: 3.44 us -> none
    pallas_call x0 -> x1, Pallas kernels: none -> 1.93 us  [on_device(): pl.pallas_call(hand_out, out_shape=shapes, in_specs=[vmem] * 2, out_specs...]
where the time goes in v3:
time: 70.7 us; the launch traced here: 70.6 us
  Pallas kernels  69.9 us (99%)
    pallas_call x1, Pallas kernels, on_device(): pl.pallas_call(functools.partial(kernel, replicas, float(rows) ** 0.5), o...  68 us
    pallas_call x1, Pallas kernels, on_device(): pl.pallas_call(hand_out, out_shape=shapes, in_specs=[vmem] * 2, out_specs...  1.93 us

profile of v3, /device:TPU:0, one launch (start us, length us, event | category | flops | bytes accessed | tf_op | source)
XLA Modules:
  0.0 70.6 jit_solution(16940685994541879599)
XLA Ops:
  0.6 68.0 %shard_map.59 = (f32[32,4096]{1,0:T(8,128)}, f32[32,1024]{1,0:T(8,128)}) custom-call(bf16[256,4096]{1,0:T(8,128)(2,1)} %cot_hbm.1, bf16[256,1024]{1,0:T(8,128)(2,1)} %act_hbm.1, bf16[2,4,512,1024]{3,2,1,0:T(8,128)(2,1)} %bitcast.1, f32[32,1024]{1,0:T(8,128)} %q_hbm.1), custom_call_target="tpu_custom_call" | custom-call | tf_op jit(solution)/shard_map/pallas_call | solution.py:302
  68.6 1.9 %shard_map.60 = (f32[32,4096]{1,0:T(8,128)}, f32[32,1024]{1,0:T(8,128)}) custom-call(f32[32,4096]{1,0:T(8,128)} %get-tuple-element.4.p_in, f32[32,1024]{1,0:T(8,128)} %get-tuple-element.5.q_in), custom_call_target="tpu_custom_call" | custom-call | tf_op jit(solution)/shard_map/pallas_call | solution.py:330
